TPU v7x, 256 devices: a whole 4x4x8 slice. The times are simulated.
256 devices in a mesh: mrow: 32 (over x_hi, z, core), mcol: 8 (over y, x_lo).
Axes of the slice: x: 4 (x_hi: 2, x_lo: 2; x = x_hi * 2 + x_lo), y: 4, z: 8, core: 2. Of those that a mesh axis runs over, the one named last changes fastest.
Arguments:
- queries: bfloat16 [4096, 4096], P('mrow', 'mcol'), may hold values from -6 to 6
- grad_out: bfloat16 [4096, 4096], P('mrow', 'mcol'), may hold values from -6 to 6
- attn_out: bfloat16 [4096, 4096], P('mrow', 'mcol'), may hold values from -2 to 2
- log_sum: float32 [4096, 32], P('mrow', 'mcol'), as said below
- memory_keys: bfloat16 [256, 128, 1024], P('mrow', 'mcol'), may hold values from -6 to 6
- memory_values: bfloat16 [256, 128, 1024], P('mrow', 'mcol'), may hold values from -6 to 6
Outputs:
- grad_queries: float32 [4096, 4096], P('mrow', 'mcol')
Inputs may be any that keep to these rules, and one draw needn't show every extreme that they name: `log_sum`: each entry is the natural logarithm of 32768, plus 0 to 1.
All inputs are finite; a program needn't handle non-finite values.
Results may differ from a plain program's by a relative error of at most 0.0023.
Values may be sent and summed in bfloat16 or wider, within the bound.
A program may use at most 64 MiB of HBM per device.

v0:
```python
import jax
import jax.numpy as jnp
from jax import lax
from jax.sharding import PartitionSpec as P

H = 32
KVH = 8
HD = 128


def divisor_at_most(total, limit):
    best = 1
    for size in range(1, total + 1):
        if total % size == 0 and size <= limit:
            best = size
    return best


def head_terms(query_heads, grad_heads, log_heads, dot_heads, mem_keys, mem_values):
    scaling = HD ** (-0.5)
    scores = (
        jnp.einsum("tkgd,ekd->kgte", query_heads, mem_keys, preferred_element_type=jnp.float32)
        * scaling
    )
    weights = jnp.exp(scores - log_heads[..., None])
    grad_probs = jnp.einsum(
        "tkgd,ekd->kgte", grad_heads, mem_values, preferred_element_type=jnp.float32
    )
    grad_scores = (weights * (grad_probs - dot_heads[..., None])).astype(jnp.bfloat16)
    return scaling * jnp.einsum(
        "kgte,ekd->tkgd", grad_scores, mem_keys, preferred_element_type=jnp.float32
    )


def block_terms(stacked, log_rows, dot_rows, mem_keys, mem_values):
    row_count = stacked.shape[0]
    heads_here = log_rows.shape[1]
    per_group = H // KVH
    kv_here = heads_here // per_group
    entries = mem_keys.shape[0]
    step = divisor_at_most(row_count, max(1, 2**21 // (heads_here * entries)))
    count = row_count // step
    query_heads = stacked[:, 0].reshape(count, step, kv_here, per_group, HD)
    grad_heads = stacked[:, 1].reshape(count, step, kv_here, per_group, HD)
    log_heads = log_rows.reshape(count, step, kv_here, per_group).transpose(0, 2, 3, 1)
    dot_heads = dot_rows.reshape(count, step, kv_here, per_group).transpose(0, 2, 3, 1)

    def one_block(inputs):
        query_part, grad_part, log_part, dot_part = inputs
        return head_terms(query_part, grad_part, log_part, dot_part, mem_keys, mem_values)

    terms = lax.map(one_block, (query_heads, grad_heads, log_heads, dot_heads))
    return terms.reshape(row_count, heads_here * HD)


def body(queries, grad_out, attn_out, log_sum, memory_keys, memory_values):
    token_count = queries.shape[0]
    heads_here = log_sum.shape[1]
    kv_here = heads_here // (H // KVH)
    out_dot = jnp.sum(
        (grad_out.astype(jnp.float32) * attn_out.astype(jnp.float32)).reshape(
            token_count, heads_here, HD
        ),
        axis=-1,
    )
    key_tiles = memory_keys.reshape(memory_keys.shape[0], memory_keys.shape[1], KVH, HD)
    value_tiles = memory_values.reshape(memory_values.shape[0], memory_values.shape[1], KVH, HD)
    own_keys, own_values = (
        lax.all_to_all(key_tiles, "mcol", split_axis=2, concat_axis=1, tiled=True),
        lax.all_to_all(value_tiles, "mcol", split_axis=2, concat_axis=1, tiled=True),
    )
    mem_keys = own_keys.reshape(-1, kv_here, HD)
    mem_values = own_values.reshape(-1, kv_here, HD)
    stacked = jnp.stack([queries, grad_out], axis=1)
    gathered_stats = (
        lax.all_gather(log_sum, "mrow", axis=0, tiled=True),
        lax.all_gather(out_dot, "mrow", axis=0, tiled=True),
    )
    log_rows = gathered_stats[0]
    dot_rows = gathered_stats[1]
    partial_grad = block_terms(
        lax.all_gather(stacked, "mrow", axis=0, tiled=True),
        log_rows,
        dot_rows,
        mem_keys,
        mem_values,
    )
    result = lax.psum_scatter(partial_grad, "mrow", scatter_dimension=0, tiled=True)
    return result


def solution(mesh):
    return jax.shard_map(
        body,
        mesh=mesh,
        in_specs=(
            P("mrow", "mcol"),
            P("mrow", "mcol"),
            P("mrow", "mcol"),
            P("mrow", "mcol"),
            P("mrow", "mcol", None),
            P("mrow", "mcol", None),
        ),
        out_specs=P("mrow", "mcol"),
        check_vma=False,
    )
```

profile of v0, /device:TPU:8, one launch (start us, length us, event | category | flops | bytes accessed | tf_op | source)
XLA Modules:
  0.0 411.1 jit_solution(14667618074723072190)
XLA Ops:
  6.5 1.7 pad_maximum_fusion
  8.3 0.8 copy_bitcast_fusion.8
  9.1 5.8 %all-to-all-start = ((bf16[8,16,8,128]{3,1,0,2:T(8,128)(2,1)}), bf16[8,16,8,128]{3,1,0,2:T(8,128)(2,1)S(1)}, u32[]{:S(2)}, u32[]{:S(2)}) async-start(bf16[8,16,8,128]{3,1,0,2:T(8,128)(2,1)} %copy_bitcast_fusion.8), calls=%async_computation | async-start | bytes 524288 | tf_op jit(solution)/shard_map/all_to_all | solution.py:69
  14.9 1.7 copy_bitcast_fusion.7
  16.6 4.1 all-to-all-done
  20.7 4.8 %all-to-all-start.1 = ((bf16[8,16,8,128]{3,1,0,2:T(8,128)(2,1)}), bf16[8,16,8,128]{3,1,0,2:T(8,128)(2,1)S(1)}, u32[]{:S(2)}, u32[]{:S(2)}) async-start(bf16[8,16,8,128]{3,1,0,2:T(8,128)(2,1)} %copy_bitcast_fusion.7), calls=%async_computation.1 | async-start | bytes 524288 | tf_op jit(solution)/shard_map/all_to_all | solution.py:70
  25.5 1.0 convert_multiply_fusion
  26.8 52.1 %all_gather.11 = f32[4096,4]{1,0:T(8,128)S(1)} all-gather(f32[128,4]{1,0:T(8,128)S(1)} %reduce_sum.9), channel_id=1, replica_groups=mesh['mrow'=32,'mcol'=8] {'mrow'}, dimensions={0}, use_global_device_ids=true | all-gather | bytes 67584 | tf_op jit(solution)/shard_map/all_gather | solution.py:77
  78.9 0.6 copy.40
  79.6 37.0 %all_gather.10 = f32[4096,4]{0,1:T(4,128)S(1)} all-gather(f32[128,4]{0,1:T(4,128)S(1)} %copy-done.1), channel_id=1, replica_groups=mesh['mrow'=32,'mcol'=8] {'mrow'}, dimensions={0}, use_global_device_ids=true | all-gather | bytes 67584 | tf_op jit(solution)/shard_map/all_gather | solution.py:76
  117.0 5.7 %fusion.20 = (bf16[4096,1,512]{2,0,1:T(8,128)(2,1)}, bf16[4096,1,512]{2,0,1:T(8,128)(2,1)}) fusion(bf16[4096,2,512]{2,0,1:T(8,128)(2,1)} %all-gather.2.cloned.1.call-done), kind=kLoop, calls=%fused_computation.28 | loop fusion | bytes 16777216 | tf_op jit(solution)/shard_map/slice | solution.py:44
  122.8 6.9 %reshape.69 = bf16[8,512,1,4,128]{4,3,1,0,2:T(4,128)(2,1)} reshape(bf16[4096,1,512]{2,0,1:T(8,128)(2,1)} %get-tuple-element.93) | data formatting | bytes 8388608 | tf_op jit(solution)/shard_map/reshape;squeeze | solution.py:43
  129.7 6.9 %reshape.70 = bf16[8,512,1,4,128]{4,3,1,0,2:T(4,128)(2,1)} reshape(bf16[4096,1,512]{2,0,1:T(8,128)(2,1)} %get-tuple-element.92) | data formatting | bytes 8388608 | tf_op jit(solution)/shard_map/reshape;squeeze | solution.py:44
  136.6 108.8 %while.10 = (s32[]{:T(128)}, f32[8,512,1,4,128]{4,3,1,0,2:T(4,128)}, bf16[8,512,1,4,128]{4,3,1,0,2:T(4,128)(2,1)}, bf16[1024,1,128]{2,0,1:T(8,128)(2,1)S(1)}, f3...) while((s32[]{:T(128)}, ...), condition=%wide.region_2.3_spmd, body=%wide.region_1.2_spmd.sunk | while | flops 1621360640 | bytes 23921256 | solution.py:52
  136.6 1.6 constant_dynamic-slice_fusion.5
  138.2 4.5 %fusion.33 = f32[512,4,1024]{2,0,1:T(8,128)} fusion(bf16[1,512,1,4,128]{4,3,1,0,2:T(4,128)(2,1)S(1)} %get-tuple-element.147, bf16[1024,1,128]{2,0,1:T(8,128)(2,1)S(1)} %get-tuple-element.172), kind=kOutput, calls=%fused_computation.13.clone.1 | convolution fusion | flops 536870912 | bytes 9175040 | tf_op jit(solution)/shard_map/while/body/eval_jaxpr/tkgd,ekd->kgte/dot_general | solution.py:22
  142.7 5.8 %fusion.34 = f32[1,512,1,4,128]{4,1,3,2,0:T(8,128)S(1)} fusion(f32[512,4,1024]{2,0,1:T(8,128)} %fusion.33, f32[4,512]{1,0:T(4,128)S(1)} %get-tuple-element.148, f32[4,512]{1,0:T(4,128)S(1)} %get-tuple-element.149, bf16[1,512,1,4,128]{4,3,1,0,2:T(4,128)(2,1)S(1)} %get-tuple-element.150, bf16[1024,1,128]{2,0,1:T(8,128)(2,1)S(1)} %get-tuple-element.175, ...), kind=kOutput, calls=%fused_computation.9.clone.1 | convolution fusion | flops 1084489728 | bytes 10502144 | tf_op jit(solution)/shard_map/while/body/eval_jaxpr/kgte,ekd->tkgd/dot_general | solution.py:30
  148.5 1.7 copy_dynamic-update-slice_fusion.2
  150.2 1.6 constant_dynamic-slice_fusion.5
  151.8 4.5 %fusion.33 = f32[512,4,1024]{2,0,1:T(8,128)} fusion(bf16[1,512,1,4,128]{4,3,1,0,2:T(4,128)(2,1)S(1)} %get-tuple-element.147, bf16[1024,1,128]{2,0,1:T(8,128)(2,1)S(1)} %get-tuple-element.172), kind=kOutput, calls=%fused_computation.13.clone.1 | convolution fusion | flops 536870912 | bytes 9175040 | tf_op jit(solution)/shard_map/while/body/eval_jaxpr/tkgd,ekd->kgte/dot_general | solution.py:22
  156.2 5.8 %fusion.34 = f32[1,512,1,4,128]{4,1,3,2,0:T(8,128)S(1)} fusion(f32[512,4,1024]{2,0,1:T(8,128)} %fusion.33, f32[4,512]{1,0:T(4,128)S(1)} %get-tuple-element.148, f32[4,512]{1,0:T(4,128)S(1)} %get-tuple-element.149, bf16[1,512,1,4,128]{4,3,1,0,2:T(4,128)(2,1)S(1)} %get-tuple-element.150, bf16[1024,1,128]{2,0,1:T(8,128)(2,1)S(1)} %get-tuple-element.175, ...), kind=kOutput, calls=%fused_computation.9.clone.1 | convolution fusion | flops 1084489728 | bytes 10502144 | tf_op jit(solution)/shard_map/while/body/eval_jaxpr/kgte,ekd->tkgd/dot_general | solution.py:30
  162.1 1.7 copy_dynamic-update-slice_fusion.2
  163.8 1.6 constant_dynamic-slice_fusion.5
  165.4 4.5 %fusion.33 = f32[512,4,1024]{2,0,1:T(8,128)} fusion(bf16[1,512,1,4,128]{4,3,1,0,2:T(4,128)(2,1)S(1)} %get-tuple-element.147, bf16[1024,1,128]{2,0,1:T(8,128)(2,1)S(1)} %get-tuple-element.172), kind=kOutput, calls=%fused_computation.13.clone.1 | convolution fusion | flops 536870912 | bytes 9175040 | tf_op jit(solution)/shard_map/while/body/eval_jaxpr/tkgd,ekd->kgte/dot_general | solution.py:22
  169.9 5.8 %fusion.34 = f32[1,512,1,4,128]{4,1,3,2,0:T(8,128)S(1)} fusion(f32[512,4,1024]{2,0,1:T(8,128)} %fusion.33, f32[4,512]{1,0:T(4,128)S(1)} %get-tuple-element.148, f32[4,512]{1,0:T(4,128)S(1)} %get-tuple-element.149, bf16[1,512,1,4,128]{4,3,1,0,2:T(4,128)(2,1)S(1)} %get-tuple-element.150, bf16[1024,1,128]{2,0,1:T(8,128)(2,1)S(1)} %get-tuple-element.175, ...), kind=kOutput, calls=%fused_computation.9.clone.1 | convolution fusion | flops 1084489728 | bytes 10502144 | tf_op jit(solution)/shard_map/while/body/eval_jaxpr/kgte,ekd->tkgd/dot_general | solution.py:30
  175.7 1.7 copy_dynamic-update-slice_fusion.2
  177.4 1.6 constant_dynamic-slice_fusion.5
  179.0 4.5 %fusion.33 = f32[512,4,1024]{2,0,1:T(8,128)} fusion(bf16[1,512,1,4,128]{4,3,1,0,2:T(4,128)(2,1)S(1)} %get-tuple-element.147, bf16[1024,1,128]{2,0,1:T(8,128)(2,1)S(1)} %get-tuple-element.172), kind=kOutput, calls=%fused_computation.13.clone.1 | convolution fusion | flops 536870912 | bytes 9175040 | tf_op jit(solution)/shard_map/while/body/eval_jaxpr/tkgd,ekd->kgte/dot_general | solution.py:22
  183.5 5.8 %fusion.34 = f32[1,512,1,4,128]{4,1,3,2,0:T(8,128)S(1)} fusion(f32[512,4,1024]{2,0,1:T(8,128)} %fusion.33, f32[4,512]{1,0:T(4,128)S(1)} %get-tuple-element.148, f32[4,512]{1,0:T(4,128)S(1)} %get-tuple-element.149, bf16[1,512,1,4,128]{4,3,1,0,2:T(4,128)(2,1)S(1)} %get-tuple-element.150, bf16[1024,1,128]{2,0,1:T(8,128)(2,1)S(1)} %get-tuple-element.175, ...), kind=kOutput, calls=%fused_computation.9.clone.1 | convolution fusion | flops 1084489728 | bytes 10502144 | tf_op jit(solution)/shard_map/while/body/eval_jaxpr/kgte,ekd->tkgd/dot_general | solution.py:30
  189.3 1.7 copy_dynamic-update-slice_fusion.2
  191.0 1.6 constant_dynamic-slice_fusion.5
  192.6 4.5 %fusion.33 = f32[512,4,1024]{2,0,1:T(8,128)} fusion(bf16[1,512,1,4,128]{4,3,1,0,2:T(4,128)(2,1)S(1)} %get-tuple-element.147, bf16[1024,1,128]{2,0,1:T(8,128)(2,1)S(1)} %get-tuple-element.172), kind=kOutput, calls=%fused_computation.13.clone.1 | convolution fusion | flops 536870912 | bytes 9175040 | tf_op jit(solution)/shard_map/while/body/eval_jaxpr/tkgd,ekd->kgte/dot_general | solution.py:22
  197.1 5.8 %fusion.34 = f32[1,512,1,4,128]{4,1,3,2,0:T(8,128)S(1)} fusion(f32[512,4,1024]{2,0,1:T(8,128)} %fusion.33, f32[4,512]{1,0:T(4,128)S(1)} %get-tuple-element.148, f32[4,512]{1,0:T(4,128)S(1)} %get-tuple-element.149, bf16[1,512,1,4,128]{4,3,1,0,2:T(4,128)(2,1)S(1)} %get-tuple-element.150, bf16[1024,1,128]{2,0,1:T(8,128)(2,1)S(1)} %get-tuple-element.175, ...), kind=kOutput, calls=%fused_computation.9.clone.1 | convolution fusion | flops 1084489728 | bytes 10502144 | tf_op jit(solution)/shard_map/while/body/eval_jaxpr/kgte,ekd->tkgd/dot_general | solution.py:30
  202.9 1.6 copy_dynamic-update-slice_fusion.2
  204.6 1.6 constant_dynamic-slice_fusion.5
  206.1 4.5 %fusion.33 = f32[512,4,1024]{2,0,1:T(8,128)} fusion(bf16[1,512,1,4,128]{4,3,1,0,2:T(4,128)(2,1)S(1)} %get-tuple-element.147, bf16[1024,1,128]{2,0,1:T(8,128)(2,1)S(1)} %get-tuple-element.172), kind=kOutput, calls=%fused_computation.13.clone.1 | convolution fusion | flops 536870912 | bytes 9175040 | tf_op jit(solution)/shard_map/while/body/eval_jaxpr/tkgd,ekd->kgte/dot_general | solution.py:22
  210.6 5.8 %fusion.34 = f32[1,512,1,4,128]{4,1,3,2,0:T(8,128)S(1)} fusion(f32[512,4,1024]{2,0,1:T(8,128)} %fusion.33, f32[4,512]{1,0:T(4,128)S(1)} %get-tuple-element.148, f32[4,512]{1,0:T(4,128)S(1)} %get-tuple-element.149, bf16[1,512,1,4,128]{4,3,1,0,2:T(4,128)(2,1)S(1)} %get-tuple-element.150, bf16[1024,1,128]{2,0,1:T(8,128)(2,1)S(1)} %get-tuple-element.175, ...), kind=kOutput, calls=%fused_computation.9.clone.1 | convolution fusion | flops 1084489728 | bytes 10502144 | tf_op jit(solution)/shard_map/while/body/eval_jaxpr/kgte,ekd->tkgd/dot_general | solution.py:30
  216.5 1.7 copy_dynamic-update-slice_fusion.2
  218.2 1.6 constant_dynamic-slice_fusion.5
  219.8 4.5 %fusion.33 = f32[512,4,1024]{2,0,1:T(8,128)} fusion(bf16[1,512,1,4,128]{4,3,1,0,2:T(4,128)(2,1)S(1)} %get-tuple-element.147, bf16[1024,1,128]{2,0,1:T(8,128)(2,1)S(1)} %get-tuple-element.172), kind=kOutput, calls=%fused_computation.13.clone.1 | convolution fusion | flops 536870912 | bytes 9175040 | tf_op jit(solution)/shard_map/while/body/eval_jaxpr/tkgd,ekd->kgte/dot_general | solution.py:22
  224.2 5.8 %fusion.34 = f32[1,512,1,4,128]{4,1,3,2,0:T(8,128)S(1)} fusion(f32[512,4,1024]{2,0,1:T(8,128)} %fusion.33, f32[4,512]{1,0:T(4,128)S(1)} %get-tuple-element.148, f32[4,512]{1,0:T(4,128)S(1)} %get-tuple-element.149, bf16[1,512,1,4,128]{4,3,1,0,2:T(4,128)(2,1)S(1)} %get-tuple-element.150, bf16[1024,1,128]{2,0,1:T(8,128)(2,1)S(1)} %get-tuple-element.175, ...), kind=kOutput, calls=%fused_computation.9.clone.1 | convolution fusion | flops 1084489728 | bytes 10502144 | tf_op jit(solution)/shard_map/while/body/eval_jaxpr/kgte,ekd->tkgd/dot_general | solution.py:30
  230.1 1.7 copy_dynamic-update-slice_fusion.2
  231.8 1.6 constant_dynamic-slice_fusion.5
  233.4 4.5 %fusion.33 = f32[512,4,1024]{2,0,1:T(8,128)} fusion(bf16[1,512,1,4,128]{4,3,1,0,2:T(4,128)(2,1)S(1)} %get-tuple-element.147, bf16[1024,1,128]{2,0,1:T(8,128)(2,1)S(1)} %get-tuple-element.172), kind=kOutput, calls=%fused_computation.13.clone.1 | convolution fusion | flops 536870912 | bytes 9175040 | tf_op jit(solution)/shard_map/while/body/eval_jaxpr/tkgd,ekd->kgte/dot_general | solution.py:22
  237.8 5.8 %fusion.34 = f32[1,512,1,4,128]{4,1,3,2,0:T(8,128)S(1)} fusion(f32[512,4,1024]{2,0,1:T(8,128)} %fusion.33, f32[4,512]{1,0:T(4,128)S(1)} %get-tuple-element.148, f32[4,512]{1,0:T(4,128)S(1)} %get-tuple-element.149, bf16[1,512,1,4,128]{4,3,1,0,2:T(4,128)(2,1)S(1)} %get-tuple-element.150, bf16[1024,1,128]{2,0,1:T(8,128)(2,1)S(1)} %get-tuple-element.175, ...), kind=kOutput, calls=%fused_computation.9.clone.1 | convolution fusion | flops 1084489728 | bytes 10502144 | tf_op jit(solution)/shard_map/while/body/eval_jaxpr/kgte,ekd->tkgd/dot_general | solution.py:30
  243.7 1.7 copy_dynamic-update-slice_fusion.2
  245.4 7.6 %copy.60 = f32[512,8,4,128]{3,1,2,0:T(8,128)} copy(f32[512,8,4,128]{3,2,1,0:T(4,128)} %bitcast.130) | data formatting | bytes 16777216
  253.0 151.2 %reduce-scatter.2.cloned.1.call-done = f32[128,512]{1,0:T(8,128)} async-done(((f32[4096,512]{1,0:T(8,128)}), f32[128,512]{1,0:T(8,128)}) %reduce-scatter.2.cloned.1.call-update) | async-done | bytes 262160 | tf_op jit(solution)/shard_map/reduce_scatter | solution.py:88
  (31 shorter events, 0.9 us)
Async XLA Ops:
  6.5 1.8 copy-start
  6.5 73.0 %copy-start.1 = (f32[128,4]{0,1:T(4,128)S(1)}, f32[128,4]{0,1:T(4,128)}, u32[]{:S(2)}) copy-start(f32[128,4]{0,1:T(4,128)} %param.11) | copy-start | bytes 6148
  6.5 110.5 %all-gather.2.cloned.1.call-start = ((), (), s32[]{:S(2)}) async-start(), calls=%async_computation.3 | async-start | bytes 8650752 | tf_op jit(solution)/shard_map/all_gather | solution.py:82
  9.1 11.6 %all-to-all-start = ((bf16[8,16,8,128]{3,1,0,2:T(8,128)(2,1)}), bf16[8,16,8,128]{3,1,0,2:T(8,128)(2,1)S(1)}, u32[]{:S(2)}, u32[]{:S(2)}) async-start(bf16[8,16,8,128]{3,1,0,2:T(8,128)(2,1)} %copy_bitcast_fusion.8), calls=%async_computation | async-start | bytes 524288 | tf_op jit(solution)/shard_map/all_to_all | solution.py:69
  20.7 95.9 %all-to-all-start.1 = ((bf16[8,16,8,128]{3,1,0,2:T(8,128)(2,1)}), bf16[8,16,8,128]{3,1,0,2:T(8,128)(2,1)S(1)}, u32[]{:S(2)}, u32[]{:S(2)}) async-start(bf16[8,16,8,128]{3,1,0,2:T(8,128)(2,1)} %copy_bitcast_fusion.7), calls=%async_computation.1 | async-start | bytes 524288 | tf_op jit(solution)/shard_map/all_to_all | solution.py:70
  25.5 378.7 %reduce-scatter.2.cloned.1.call-start = ((), (), s32[]{:S(2)}) async-start(), calls=%async_computation.4 | async-start | bytes 8650752 | tf_op jit(solution)/shard_map/reduce_scatter | solution.py:88
Sparse Core Ops, SparseCore 0:
  10.2 106.8 all-gather.1
  253.1 151.0 reduce-scatter.1
where the time goes:
time: 412 us; the launch traced here: 411 us
  waiting for transfers between devices  156 us (38%)
  blocking collectives  89.1 us (22%)
  matrix products  82.5 us (20%)
  local copies, waits for them, and re-layouts  56.5 us (14%)
  between operations  13.5 us (3%)
  starting transfers between devices  10.7 us (3%)
    reduce_scatter x1, waiting for transfers between devices, body(): lax.psum_scatter(partial_grad, 'mrow', scatter_dimension=0, tiled=True)  151 us
    all_gather x1, blocking collectives, body(): lax.all_gather(out_dot, 'mrow', axis=0, tiled=True)  52.1 us
    dot_general x8, matrix products, head_terms(): jnp.einsum('kgte,ekd->tkgd', grad_scores, mem_keys, preferred_element_typ...  46.7 us
    all_gather x1, blocking collectives, body(): lax.all_gather(log_sum, 'mrow', axis=0, tiled=True)  37 us
    dot_general x8, matrix products, head_terms(): jnp.einsum('tkgd,ekd->kgte', query_heads, mem_keys, preferred_element_typ...  35.8 us
    dynamic_update_slice x8, local copies, waits for them, and re-layouts, block_terms(): terms = lax.map(one_block, (query_heads, grad_heads, log_heads, dot_heads))  13.4 us
    dynamic_slice x16, local copies, waits for them, and re-layouts, block_terms(): terms = lax.map(one_block, (query_heads, grad_heads, log_heads, dot_heads))  12.6 us
  transfers between devices with their start and end apart: 4, of which 3 were waited for; matrix products, arithmetic and copies ran while one was open for 1% of the time, Pallas kernels for 0%

commit v1 on v0

--- a/solution.py
+++ b/solution.py
@@ -74,7 +74,9 @@
     stacked = jnp.stack([queries, grad_out], axis=1)
     gathered_stats = (
         lax.all_gather(log_sum, "mrow", axis=0, tiled=True),
-        lax.all_gather(out_dot, "mrow", axis=0, tiled=True),
+        jnp.concatenate(
+            lax.all_to_all(jnp.stack([out_dot] * lax.axis_size("mrow")), "mrow", 0, 0), axis=0
+        ),
     )
     log_rows = gathered_stats[0]
     dot_rows = gathered_stats[1]

time: 412 us -> 409 us (level)
  blocking collectives: 89.1 us -> 38.1 us
  waiting for transfers between devices: 156 us -> 193 us
  starting transfers between devices: 10.7 us -> 21.4 us
    all_gather x1 -> x0, blocking collectives: 52.1 us -> none  [body(): lax.all_gather(out_dot, 'mrow', axis=0, tiled=True)]
    all_gather x1, waiting for transfers between devices: 0.39 us -> 28.6 us  [body(): lax.all_gather(stacked, 'mrow', axis=0, tiled=True)]
    all_to_all x0 -> x1, starting transfers between devices: none -> 11.3 us  [body(): lax.all_to_all(jnp.stack([out_dot] * lax.axis_size('mrow')), 'mrow', 0, 0)]
    all_to_all x0 -> x1, waiting for transfers between devices: none -> 9.92 us  [body(): lax.all_to_all(jnp.stack([out_dot] * lax.axis_size('mrow')), 'mrow', 0, 0)]
  transfers between devices with their start and end apart: 4 -> 5, of which waited for: 3 -> 4; matrix products, arithmetic and copies ran while one was open for 1% -> 1% of each run, Pallas kernels for 0% -> 0%
where the time goes in v1:
time: 409 us; the launch traced here: 408 us
  waiting for transfers between devices  193 us (47%)
  matrix products  82.5 us (20%)
  local copies, waits for them, and re-layouts  56.6 us (14%)
  blocking collectives  38.1 us (9%)
  starting transfers between devices  21.4 us (5%)
  between operations  13.5 us (3%)
    reduce_scatter x1, waiting for transfers between devices, body(): lax.psum_scatter(partial_grad, 'mrow', scatter_dimension=0, tiled=True)  151 us
    dot_general x8, matrix products, head_terms(): jnp.einsum('kgte,ekd->tkgd', grad_scores, mem_keys, preferred_element_typ...  46.7 us
    all_gather x1, blocking collectives, body(): lax.all_gather(log_sum, 'mrow', axis=0, tiled=True)  38.1 us
    dot_general x8, matrix products, head_terms(): jnp.einsum('tkgd,ekd->kgte', query_heads, mem_keys, preferred_element_typ...  35.8 us
    all_gather x1, waiting for transfers between devices, body(): lax.all_gather(stacked, 'mrow', axis=0, tiled=True)  28.6 us
    dynamic_update_slice x8, local copies, waits for them, and re-layouts, block_terms(): terms = lax.map(one_block, (query_heads, grad_heads, log_heads, dot_heads))  13.4 us
    dynamic_slice x16, local copies, waits for them, and re-layouts, block_terms(): terms = lax.map(one_block, (query_heads, grad_heads, log_heads, dot_heads))  12.6 us
    all_to_all x1, starting transfers between devices, body(): lax.all_to_all(jnp.stack([out_dot] * lax.axis_size('mrow')), 'mrow', 0, 0)  11.3 us
  transfers between devices with their start and end apart: 5, of which 4 were waited for; matrix products, arithmetic and copies ran while one was open for 1% of the time, Pallas kernels for 0%

profile of v1, /device:TPU:8, one launch (start us, length us, event | category | flops | bytes accessed | tf_op | source)
XLA Modules:
  0.0 408.2 jit_solution(15209784991498231551)
XLA Ops:
  6.5 1.7 pad_maximum_fusion
  8.3 1.0 convert_multiply_fusion
  10.3 11.3 %all-to-all-start.2 = ((f32[32,128,4]{1,2,0:T(4,128)}), f32[32,128,4]{1,2,0:T(4,128)S(1)}, u32[]{:S(2)}, u32[]{:S(2)}) async-start(f32[32,128,4]{1,2,0:T(4,128)} %stack.11), calls=%async_computation.2 | async-start | bytes 131072 | tf_op jit(solution)/shard_map/all_to_all | solution.py:78
  22.4 9.9 %all-to-all-done.2 = f32[32,128,4]{1,2,0:T(4,128)S(1)} async-done(((f32[32,128,4]{1,2,0:T(4,128)}), f32[32,128,4]{1,2,0:T(4,128)S(1)}, u32[]{:S(2)}, u32[]{:S(2)}) %all-to-all-start.2) | async-done | bytes 65568 | tf_op jit(solution)/shard_map/all_to_all | solution.py:78
  32.3 4.9 %all-to-all-start = ((bf16[8,16,8,128]{3,1,0,2:T(8,128)(2,1)}), bf16[8,16,8,128]{3,1,0,2:T(8,128)(2,1)S(1)}, u32[]{:S(2)}, u32[]{:S(2)}) async-start(bf16[8,16,8,128]{3,1,0,2:T(8,128)(2,1)} %copy_bitcast_fusion.8), calls=%async_computation | async-start | bytes 524288 | tf_op jit(solution)/shard_map/all_to_all | solution.py:69
  37.3 1.7 copy_bitcast_fusion.7
  39.0 3.8 all-to-all-done
  42.8 5.1 %all-to-all-start.1 = ((bf16[8,16,8,128]{3,1,0,2:T(8,128)(2,1)}), bf16[8,16,8,128]{3,1,0,2:T(8,128)(2,1)S(1)}, u32[]{:S(2)}, u32[]{:S(2)}) async-start(bf16[8,16,8,128]{3,1,0,2:T(8,128)(2,1)} %copy_bitcast_fusion.7), calls=%async_computation.1 | async-start | bytes 524288 | tf_op jit(solution)/shard_map/all_to_all | solution.py:70
  47.9 38.1 %all_gather.7 = f32[4096,4]{0,1:T(4,128)S(1)} all-gather(f32[128,4]{0,1:T(4,128)} %param.11), channel_id=1, replica_groups=mesh['mrow'=32,'mcol'=8] {'mrow'}, dimensions={0}, use_global_device_ids=true | all-gather | bytes 67584 | tf_op jit(solution)/shard_map/all_gather | solution.py:76
  86.1 28.6 %all-gather.2.cloned.1.call-done = bf16[4096,2,512]{2,0,1:T(8,128)(2,1)} async-done(((bf16[128,2,512]{2,0,1:T(8,128)(2,1)}), bf16[4096,2,512]{2,0,1:T(8,128)(2,1)}) %all-gather.2.cloned.1.call-update) | async-done | bytes 8388624 | tf_op jit(solution)/shard_map/all_gather | solution.py:84
  114.7 5.7 %fusion.20 = (bf16[4096,1,512]{2,0,1:T(8,128)(2,1)}, bf16[4096,1,512]{2,0,1:T(8,128)(2,1)}) fusion(bf16[4096,2,512]{2,0,1:T(8,128)(2,1)} %all-gather.2.cloned.1.call-done), kind=kLoop, calls=%fused_computation.28 | loop fusion | bytes 16777216 | tf_op jit(solution)/shard_map/slice | solution.py:44
  120.4 6.9 %reshape.67 = bf16[8,512,1,4,128]{4,3,1,0,2:T(4,128)(2,1)} reshape(bf16[4096,1,512]{2,0,1:T(8,128)(2,1)} %get-tuple-element.93) | data formatting | bytes 8388608 | tf_op jit(solution)/shard_map/reshape;squeeze | solution.py:43
  127.3 6.9 %reshape.68 = bf16[8,512,1,4,128]{4,3,1,0,2:T(4,128)(2,1)} reshape(bf16[4096,1,512]{2,0,1:T(8,128)(2,1)} %get-tuple-element.92) | data formatting | bytes 8388608 | tf_op jit(solution)/shard_map/reshape;squeeze | solution.py:44
  134.3 108.8 %while.10 = (s32[]{:T(128)}, f32[8,512,1,4,128]{4,3,1,0,2:T(4,128)}, bf16[8,512,1,4,128]{4,3,1,0,2:T(4,128)(2,1)}, bf16[1024,1,128]{2,0,1:T(8,128)(2,1)S(1)}, f3...) while((s32[]{:T(128)}, ...), condition=%wide.region_2.3_spmd, body=%wide.region_1.2_spmd.sunk | while | flops 1621360640 | bytes 23921256 | solution.py:52
  134.3 1.6 constant_dynamic-slice_fusion.5
  135.9 4.5 %fusion.33 = f32[512,4,1024]{2,0,1:T(8,128)} fusion(bf16[1,512,1,4,128]{4,3,1,0,2:T(4,128)(2,1)S(1)} %get-tuple-element.147, bf16[1024,1,128]{2,0,1:T(8,128)(2,1)S(1)} %get-tuple-element.172), kind=kOutput, calls=%fused_computation.13.clone.1 | convolution fusion | flops 536870912 | bytes 9175040 | tf_op jit(solution)/shard_map/while/body/eval_jaxpr/tkgd,ekd->kgte/dot_general | solution.py:22
  140.3 5.8 %fusion.34 = f32[1,512,1,4,128]{4,1,3,2,0:T(8,128)S(1)} fusion(f32[512,4,1024]{2,0,1:T(8,128)} %fusion.33, f32[4,512]{1,0:T(4,128)S(1)} %get-tuple-element.148, f32[4,512]{1,0:T(4,128)S(1)} %get-tuple-element.149, bf16[1,512,1,4,128]{4,3,1,0,2:T(4,128)(2,1)S(1)} %get-tuple-element.150, bf16[1024,1,128]{2,0,1:T(8,128)(2,1)S(1)} %get-tuple-element.175, ...), kind=kOutput, calls=%fused_computation.9.clone.1 | convolution fusion | flops 1084489728 | bytes 10502144 | tf_op jit(solution)/shard_map/while/body/eval_jaxpr/kgte,ekd->tkgd/dot_general | solution.py:30
  146.2 1.7 copy_dynamic-update-slice_fusion.2
  147.9 1.6 constant_dynamic-slice_fusion.5
  149.4 4.5 %fusion.33 = f32[512,4,1024]{2,0,1:T(8,128)} fusion(bf16[1,512,1,4,128]{4,3,1,0,2:T(4,128)(2,1)S(1)} %get-tuple-element.147, bf16[1024,1,128]{2,0,1:T(8,128)(2,1)S(1)} %get-tuple-element.172), kind=kOutput, calls=%fused_computation.13.clone.1 | convolution fusion | flops 536870912 | bytes 9175040 | tf_op jit(solution)/shard_map/while/body/eval_jaxpr/tkgd,ekd->kgte/dot_general | solution.py:22
  153.9 5.8 %fusion.34 = f32[1,512,1,4,128]{4,1,3,2,0:T(8,128)S(1)} fusion(f32[512,4,1024]{2,0,1:T(8,128)} %fusion.33, f32[4,512]{1,0:T(4,128)S(1)} %get-tuple-element.148, f32[4,512]{1,0:T(4,128)S(1)} %get-tuple-element.149, bf16[1,512,1,4,128]{4,3,1,0,2:T(4,128)(2,1)S(1)} %get-tuple-element.150, bf16[1024,1,128]{2,0,1:T(8,128)(2,1)S(1)} %get-tuple-element.175, ...), kind=kOutput, calls=%fused_computation.9.clone.1 | convolution fusion | flops 1084489728 | bytes 10502144 | tf_op jit(solution)/shard_map/while/body/eval_jaxpr/kgte,ekd->tkgd/dot_general | solution.py:30
  159.8 1.7 copy_dynamic-update-slice_fusion.2
  161.5 1.6 constant_dynamic-slice_fusion.5
  163.0 4.5 %fusion.33 = f32[512,4,1024]{2,0,1:T(8,128)} fusion(bf16[1,512,1,4,128]{4,3,1,0,2:T(4,128)(2,1)S(1)} %get-tuple-element.147, bf16[1024,1,128]{2,0,1:T(8,128)(2,1)S(1)} %get-tuple-element.172), kind=kOutput, calls=%fused_computation.13.clone.1 | convolution fusion | flops 536870912 | bytes 9175040 | tf_op jit(solution)/shard_map/while/body/eval_jaxpr/tkgd,ekd->kgte/dot_general | solution.py:22
  167.5 5.8 %fusion.34 = f32[1,512,1,4,128]{4,1,3,2,0:T(8,128)S(1)} fusion(f32[512,4,1024]{2,0,1:T(8,128)} %fusion.33, f32[4,512]{1,0:T(4,128)S(1)} %get-tuple-element.148, f32[4,512]{1,0:T(4,128)S(1)} %get-tuple-element.149, bf16[1,512,1,4,128]{4,3,1,0,2:T(4,128)(2,1)S(1)} %get-tuple-element.150, bf16[1024,1,128]{2,0,1:T(8,128)(2,1)S(1)} %get-tuple-element.175, ...), kind=kOutput, calls=%fused_computation.9.clone.1 | convolution fusion | flops 1084489728 | bytes 10502144 | tf_op jit(solution)/shard_map/while/body/eval_jaxpr/kgte,ekd->tkgd/dot_general | solution.py:30
  173.4 1.7 copy_dynamic-update-slice_fusion.2
  175.1 1.6 constant_dynamic-slice_fusion.5
  176.6 4.5 %fusion.33 = f32[512,4,1024]{2,0,1:T(8,128)} fusion(bf16[1,512,1,4,128]{4,3,1,0,2:T(4,128)(2,1)S(1)} %get-tuple-element.147, bf16[1024,1,128]{2,0,1:T(8,128)(2,1)S(1)} %get-tuple-element.172), kind=kOutput, calls=%fused_computation.13.clone.1 | convolution fusion | flops 536870912 | bytes 9175040 | tf_op jit(solution)/shard_map/while/body/eval_jaxpr/tkgd,ekd->kgte/dot_general | solution.py:22
  181.1 5.8 %fusion.34 = f32[1,512,1,4,128]{4,1,3,2,0:T(8,128)S(1)} fusion(f32[512,4,1024]{2,0,1:T(8,128)} %fusion.33, f32[4,512]{1,0:T(4,128)S(1)} %get-tuple-element.148, f32[4,512]{1,0:T(4,128)S(1)} %get-tuple-element.149, bf16[1,512,1,4,128]{4,3,1,0,2:T(4,128)(2,1)S(1)} %get-tuple-element.150, bf16[1024,1,128]{2,0,1:T(8,128)(2,1)S(1)} %get-tuple-element.175, ...), kind=kOutput, calls=%fused_computation.9.clone.1 | convolution fusion | flops 1084489728 | bytes 10502144 | tf_op jit(solution)/shard_map/while/body/eval_jaxpr/kgte,ekd->tkgd/dot_general | solution.py:30
  187.0 1.7 copy_dynamic-update-slice_fusion.2
  188.7 1.6 constant_dynamic-slice_fusion.5
  190.2 4.5 %fusion.33 = f32[512,4,1024]{2,0,1:T(8,128)} fusion(bf16[1,512,1,4,128]{4,3,1,0,2:T(4,128)(2,1)S(1)} %get-tuple-element.147, bf16[1024,1,128]{2,0,1:T(8,128)(2,1)S(1)} %get-tuple-element.172), kind=kOutput, calls=%fused_computation.13.clone.1 | convolution fusion | flops 536870912 | bytes 9175040 | tf_op jit(solution)/shard_map/while/body/eval_jaxpr/tkgd,ekd->kgte/dot_general | solution.py:22
  194.7 5.8 %fusion.34 = f32[1,512,1,4,128]{4,1,3,2,0:T(8,128)S(1)} fusion(f32[512,4,1024]{2,0,1:T(8,128)} %fusion.33, f32[4,512]{1,0:T(4,128)S(1)} %get-tuple-element.148, f32[4,512]{1,0:T(4,128)S(1)} %get-tuple-element.149, bf16[1,512,1,4,128]{4,3,1,0,2:T(4,128)(2,1)S(1)} %get-tuple-element.150, bf16[1024,1,128]{2,0,1:T(8,128)(2,1)S(1)} %get-tuple-element.175, ...), kind=kOutput, calls=%fused_computation.9.clone.1 | convolution fusion | flops 1084489728 | bytes 10502144 | tf_op jit(solution)/shard_map/while/body/eval_jaxpr/kgte,ekd->tkgd/dot_general | solution.py:30
  200.6 1.7 copy_dynamic-update-slice_fusion.2
  202.2 1.6 constant_dynamic-slice_fusion.5
  203.8 4.5 %fusion.33 = f32[512,4,1024]{2,0,1:T(8,128)} fusion(bf16[1,512,1,4,128]{4,3,1,0,2:T(4,128)(2,1)S(1)} %get-tuple-element.147, bf16[1024,1,128]{2,0,1:T(8,128)(2,1)S(1)} %get-tuple-element.172), kind=kOutput, calls=%fused_computation.13.clone.1 | convolution fusion | flops 536870912 | bytes 9175040 | tf_op jit(solution)/shard_map/while/body/eval_jaxpr/tkgd,ekd->kgte/dot_general | solution.py:22
  208.3 5.8 %fusion.34 = f32[1,512,1,4,128]{4,1,3,2,0:T(8,128)S(1)} fusion(f32[512,4,1024]{2,0,1:T(8,128)} %fusion.33, f32[4,512]{1,0:T(4,128)S(1)} %get-tuple-element.148, f32[4,512]{1,0:T(4,128)S(1)} %get-tuple-element.149, bf16[1,512,1,4,128]{4,3,1,0,2:T(4,128)(2,1)S(1)} %get-tuple-element.150, bf16[1024,1,128]{2,0,1:T(8,128)(2,1)S(1)} %get-tuple-element.175, ...), kind=kOutput, calls=%fused_computation.9.clone.1 | convolution fusion | flops 1084489728 | bytes 10502144 | tf_op jit(solution)/shard_map/while/body/eval_jaxpr/kgte,ekd->tkgd/dot_general | solution.py:30
  214.1 1.7 copy_dynamic-update-slice_fusion.2
  215.8 1.6 constant_dynamic-slice_fusion.5
  217.4 4.5 %fusion.33 = f32[512,4,1024]{2,0,1:T(8,128)} fusion(bf16[1,512,1,4,128]{4,3,1,0,2:T(4,128)(2,1)S(1)} %get-tuple-element.147, bf16[1024,1,128]{2,0,1:T(8,128)(2,1)S(1)} %get-tuple-element.172), kind=kOutput, calls=%fused_computation.13.clone.1 | convolution fusion | flops 536870912 | bytes 9175040 | tf_op jit(solution)/shard_map/while/body/eval_jaxpr/tkgd,ekd->kgte/dot_general | solution.py:22
  221.9 5.8 %fusion.34 = f32[1,512,1,4,128]{4,1,3,2,0:T(8,128)S(1)} fusion(f32[512,4,1024]{2,0,1:T(8,128)} %fusion.33, f32[4,512]{1,0:T(4,128)S(1)} %get-tuple-element.148, f32[4,512]{1,0:T(4,128)S(1)} %get-tuple-element.149, bf16[1,512,1,4,128]{4,3,1,0,2:T(4,128)(2,1)S(1)} %get-tuple-element.150, bf16[1024,1,128]{2,0,1:T(8,128)(2,1)S(1)} %get-tuple-element.175, ...), kind=kOutput, calls=%fused_computation.9.clone.1 | convolution fusion | flops 1084489728 | bytes 10502144 | tf_op jit(solution)/shard_map/while/body/eval_jaxpr/kgte,ekd->tkgd/dot_general | solution.py:30
  227.7 1.7 copy_dynamic-update-slice_fusion.2
  229.4 1.6 constant_dynamic-slice_fusion.5
  231.0 4.5 %fusion.33 = f32[512,4,1024]{2,0,1:T(8,128)} fusion(bf16[1,512,1,4,128]{4,3,1,0,2:T(4,128)(2,1)S(1)} %get-tuple-element.147, bf16[1024,1,128]{2,0,1:T(8,128)(2,1)S(1)} %get-tuple-element.172), kind=kOutput, calls=%fused_computation.13.clone.1 | convolution fusion | flops 536870912 | bytes 9175040 | tf_op jit(solution)/shard_map/while/body/eval_jaxpr/tkgd,ekd->kgte/dot_general | solution.py:22
  235.5 5.8 %fusion.34 = f32[1,512,1,4,128]{4,1,3,2,0:T(8,128)S(1)} fusion(f32[512,4,1024]{2,0,1:T(8,128)} %fusion.33, f32[4,512]{1,0:T(4,128)S(1)} %get-tuple-element.148, f32[4,512]{1,0:T(4,128)S(1)} %get-tuple-element.149, bf16[1,512,1,4,128]{4,3,1,0,2:T(4,128)(2,1)S(1)} %get-tuple-element.150, bf16[1024,1,128]{2,0,1:T(8,128)(2,1)S(1)} %get-tuple-element.175, ...), kind=kOutput, calls=%fused_computation.9.clone.1 | convolution fusion | flops 1084489728 | bytes 10502144 | tf_op jit(solution)/shard_map/while/body/eval_jaxpr/kgte,ekd->tkgd/dot_general | solution.py:30
  241.3 1.7 copy_dynamic-update-slice_fusion.2
  243.0 7.6 %copy.61 = f32[512,8,4,128]{3,1,2,0:T(8,128)} copy(f32[512,8,4,128]{3,2,1,0:T(4,128)} %bitcast.131) | data formatting | bytes 16777216
  250.6 150.7 %reduce-scatter.2.cloned.1.call-done = f32[128,512]{1,0:T(8,128)} async-done(((f32[4096,512]{1,0:T(8,128)}), f32[128,512]{1,0:T(8,128)}) %reduce-scatter.2.cloned.1.call-update) | async-done | bytes 262160 | tf_op jit(solution)/shard_map/reduce_scatter | solution.py:90
  (33 shorter events, 2.0 us)
Async XLA Ops:
  6.5 15.1 %copy-start = (bf16[8,16,1024]{2,1,0:T(8,128)(2,1)S(1)}, bf16[8,16,1024]{2,1,0:T(8,128)(2,1)}, u32[]{:S(2)}) copy-start(bf16[8,16,1024]{2,1,0:T(8,128)(2,1)} %param.12) | copy-start | bytes 786436
  6.5 108.2 %all-gather.2.cloned.1.call-start = ((), (), s32[]{:S(2)}) async-start(), calls=%async_computation.4 | async-start | bytes 8650752 | tf_op jit(solution)/shard_map/all_gather | solution.py:84
  10.3 22.0 %all-to-all-start.2 = ((f32[32,128,4]{1,2,0:T(4,128)}), f32[32,128,4]{1,2,0:T(4,128)S(1)}, u32[]{:S(2)}, u32[]{:S(2)}) async-start(f32[32,128,4]{1,2,0:T(4,128)} %stack.11), calls=%async_computation.2 | async-start | bytes 131072 | tf_op jit(solution)/shard_map/all_to_all | solution.py:78
  32.3 10.5 %all-to-all-start = ((bf16[8,16,8,128]{3,1,0,2:T(8,128)(2,1)}), bf16[8,16,8,128]{3,1,0,2:T(8,128)(2,1)S(1)}, u32[]{:S(2)}, u32[]{:S(2)}) async-start(bf16[8,16,8,128]{3,1,0,2:T(8,128)(2,1)} %copy_bitcast_fusion.8), calls=%async_computation | async-start | bytes 524288 | tf_op jit(solution)/shard_map/all_to_all | solution.py:69
  42.8 43.3 %all-to-all-start.1 = ((bf16[8,16,8,128]{3,1,0,2:T(8,128)(2,1)}), bf16[8,16,8,128]{3,1,0,2:T(8,128)(2,1)S(1)}, u32[]{:S(2)}, u32[]{:S(2)}) async-start(bf16[8,16,8,128]{3,1,0,2:T(8,128)(2,1)} %copy_bitcast_fusion.7), calls=%async_computation.1 | async-start | bytes 524288 | tf_op jit(solution)/shard_map/all_to_all | solution.py:70
  47.9 353.4 %reduce-scatter.2.cloned.1.call-start = ((), (), s32[]{:S(2)}) async-start(), calls=%async_computation.5 | async-start | bytes 8650752 | tf_op jit(solution)/shard_map/reduce_scatter | solution.py:90
Sparse Core Ops, SparseCore 0:
  10.2 104.4 all-gather.1
  250.8 150.5 reduce-scatter.1
